TPU v7x, 256 devices: a whole 4x4x8 slice. The times are simulated.
256 devices in a mesh: dp: 4 (over z_lo, core), seq: 64 (over z_hi, y, x).
Axes of the slice: x: 4, y: 4, z: 8 (z_hi: 4, z_lo: 2; z = z_hi * 2 + z_lo), core: 2. Of those that a mesh axis runs over, the one named last changes fastest.
Arguments:
- glu_out: bfloat16 [4, 8192, 1536], P('dp', 'seq'), may hold values from -6 to 6
- lengths: int32 [4], replicated, may hold values from 1024 to 8192, as said below
- kernel: float32 [31, 1536], replicated, may hold values from -1 to 1
- gain: float32 [1536], replicated, may hold values from 0.25 to 1.75
- bias: float32 [1536], replicated, may hold values from -3 to 3
- weight: bfloat16 [1536, 1536], P(('dp', 'seq')), may hold values from -0.15625 to 0.15625
- master: float32 [1536, 1536], P(('dp', 'seq')), may hold values from -0.15625 to 0.15625
- moment_one: float32 [1536, 1536], P(('dp', 'seq')), may hold values from -120 to 120
- moment_two: float32 [1536, 1536], P(('dp', 'seq')), may hold values from 100 to 100000
- cotangent: bfloat16 [4, 8192, 1536], P('dp', 'seq'), may hold values from -6 to 6
Outputs:
- module_out: bfloat16 [4, 8192, 1536], P('dp', 'seq')
- input_grad: bfloat16 [4, 8192, 1536], P('dp', 'seq')
- kernel_grad: float32 [31, 1536], replicated
- gain_grad: float32 [1536], replicated
- bias_grad: float32 [1536], replicated
- new_master: float32 [1536, 1536], P(('dp', 'seq'))
- new_one: float32 [1536, 1536], P(('dp', 'seq'))
- new_two: float32 [1536, 1536], P(('dp', 'seq'))
Inputs may be any that keep to these rules, and one draw needn't show every extreme that they name: `lengths`: in every draw one stream has all 8192 frames valid; each other stream has between 1024 and 2730 valid frames.
All inputs are finite; a program needn't handle non-finite values.
Results may differ from a plain program's by a relative error of at most 0.0049.
Values may be sent and summed in bfloat16 or wider, within the bound.
No kernel may reach another device: no remote copies, remote signals or barrier semaphores. Data moves between devices by JAX's collectives and lax.ppermute only.
A program may use at most 64 MiB of HBM per device.

v0:
```python
import jax
import jax.numpy as jnp
from jax import lax
from jax.sharding import PartitionSpec as P

KERNEL = 31
HALF = 15
beta_one = 0.9
beta_two = 0.999
adam_rate = 0.001
adam_eps = 1e-08
norm_eps = 1e-05
first_fix = 0.9999734386011124
second_fix = 0.09520785288629043


def with_halo(block, sides, width):
    for axis, dim in sides:
        count = lax.axis_size(axis)
        forward = [(i, i + 1) for i in range(count - 1)]
        backward = [(target, source) for source, target in forward]
        low = lax.ppermute(
            lax.slice_in_dim(block, block.shape[dim] - width, None, axis=dim), axis, forward
        )
        high = lax.ppermute(lax.slice_in_dim(block, 0, width, axis=dim), axis, backward)
        block = jnp.concatenate([low, block, high], axis=dim)
    return block


def on_device(
    glu_out, lengths, kernel, gain, bias, weight, master, moment_one, moment_two, cotangent
):
    frames = glu_out.shape[1]
    stream = lax.axis_index("dp")
    shard = lax.axis_index("seq")
    positions = shard * frames + jnp.arange(frames, dtype=jnp.int32)
    valid = (positions < lengths[stream])[:, None]
    count = jnp.sum(lengths).astype(jnp.float32)
    masked = jnp.where(valid, glu_out[0], jnp.zeros((), glu_out.dtype))
    padded = with_halo(masked, (("seq", 0),), HALF).astype(jnp.float32)
    conv_out = jnp.zeros((frames, masked.shape[1]), jnp.float32)
    for tap in range(KERNEL):
        conv_out = conv_out + kernel[tap] * padded[tap : tap + frames]
    total = lax.psum(jnp.sum(jnp.where(valid, conv_out, 0.0), axis=0), ("dp", "seq"))
    channel_mean = total / count
    deviation = jnp.where(valid, conv_out - channel_mean, 0.0)
    spread = lax.psum(jnp.sum(deviation * deviation, axis=0), ("dp", "seq"))
    channel_var = spread / count
    inv_std = lax.rsqrt(channel_var + norm_eps)
    standard = (conv_out - channel_mean) * inv_std
    scaled = gain * standard + bias
    logistic = jax.nn.sigmoid(scaled)
    hidden = (scaled * logistic).astype(jnp.bfloat16)
    grad_out = jnp.where(valid, cotangent[0], jnp.zeros((), cotangent.dtype))
    columns = hidden
    product = jnp.dot(
        columns,
        lax.all_gather(weight, ("dp", "seq"), axis=0, tiled=True),
        preferred_element_type=jnp.float32,
    )
    hidden_grad = lax.dot_general(
        grad_out,
        lax.all_gather(weight, ("dp", "seq"), axis=0, tiled=True),
        (((1,), (1,)), ((), ())),
        preferred_element_type=jnp.float32,
    )
    module_out = jnp.where(valid, product, 0.0).astype(jnp.bfloat16)
    scaled_grad = hidden_grad * logistic * (1.0 + scaled * (1.0 - logistic))
    gain_grad, bias_grad = lax.psum(
        (jnp.sum(scaled_grad * standard, axis=0), jnp.sum(scaled_grad, axis=0)), ("dp", "seq")
    )
    conv_grad = jnp.where(
        valid,
        inv_std
        * (gain * scaled_grad - gain * bias_grad / count - standard * gain * gain_grad / count),
        0.0,
    )
    grad_pad = with_halo(conv_grad, (("seq", 0),), HALF)
    flipped = jnp.zeros((frames, conv_grad.shape[1]), jnp.float32)
    for tap in range(KERNEL):
        flipped = flipped + kernel[tap] * grad_pad[2 * HALF - tap : 2 * HALF - tap + frames]
    input_grad = jnp.where(valid, flipped, 0.0).astype(jnp.bfloat16)
    tap_rows = []
    for tap in range(KERNEL):
        tap_rows.append(jnp.sum(conv_grad * padded[tap : tap + frames], axis=0))
    kernel_grad = lax.psum(jnp.stack(tap_rows), ("dp", "seq"))
    columns = hidden
    weight_grad = lax.psum_scatter(
        lax.dot_general(
            columns, grad_out, (((0,), (0,)), ((), ())), preferred_element_type=jnp.float32
        ),
        ("dp", "seq"),
        scatter_dimension=0,
        tiled=True,
    )
    new_one = beta_one * moment_one + (1.0 - beta_one) * weight_grad
    new_two = beta_two * moment_two + (1.0 - beta_two) * weight_grad * weight_grad
    new_master = master - adam_rate * (new_one / first_fix) / (
        jnp.sqrt(new_two / second_fix) + adam_eps
    )
    return (
        module_out[None],
        input_grad[None],
        kernel_grad,
        gain_grad,
        bias_grad,
        new_master,
        new_one,
        new_two,
    )


def solution(mesh):
    return jax.shard_map(
        on_device,
        mesh=mesh,
        in_specs=(
            P("dp", "seq", None),
            P(),
            P(),
            P(),
            P(),
            P(("dp", "seq"), None),
            P(("dp", "seq"), None),
            P(("dp", "seq"), None),
            P(("dp", "seq"), None),
            P("dp", "seq", None),
        ),
        out_specs=(
            P("dp", "seq", None),
            P("dp", "seq", None),
            P(),
            P(),
            P(),
            P(("dp", "seq"), None),
            P(("dp", "seq"), None),
            P(("dp", "seq"), None),
        ),
        check_vma=False,
    )
```

profile of v0, /device:TPU:1, one launch (start us, length us, event | category | flops | bytes accessed | tf_op | source)
XLA Modules:
  0.0 2008.2 jit_solution(8663492157685845760)
XLA Ops:
  12.3 4.6 collective-permute-start
  25.6 85.3 %psum.35 = f32[1536]{0:T(1024)S(1)} all-reduce(f32[1536]{0:T(1024)S(1)} %get-tuple-element.78), channel_id=1, replica_groups=mesh['dp'=4,'seq'=64] {'dp','seq'}, use_global_device_ids=true, to_apply=%region_1.2 | all-reduce | flops 1536 | bytes 12288 | tf_op jit(solution)/shard_map/psum | solution.py:44
  111.1 73.7 %psum.36 = f32[1536]{0:T(1024)S(1)} all-reduce(f32[1536]{0:T(1024)S(1)} %multiply_reduce_fusion.32), channel_id=1, replica_groups=mesh['dp'=4,'seq'=64] {'dp','seq'}, use_global_device_ids=true, to_apply=%region_4.5 | all-reduce | flops 1536 | bytes 12288 | tf_op jit(solution)/shard_map/psum | solution.py:47
  184.9 5.1 fusion.95
  190.0 808.0 %fusion = f32[8,1536]{1,0:T(8,128)S(1)} fusion(f32[1536,1536]{1,0:T(8,128)} %fusion.95), kind=kCustom, calls=%all-reduce-scatter | all-reduce-scatter fusion | flops 3145729 | bytes 9486336
  998.0 48.1 %collective-permute-start.66 = (f32[8,1536]{1,0:T(8,128)S(1)}, f32[8,1536]{1,0:T(8,128)S(1)}, u32[]{:S(2)}, u32[]{:S(2)}) collective-permute-start(f32[8,1536]{1,0:T(8,128)S(1)} %fusion), channel_id=1, source_target_pairs={{0,63},{1,64},{2,65},{3,66},{4,67},{5,68},{6,69},{7,70},{8,71},{9,... | collective-permute-start | bytes 147464
  1050.0 4.0 collective-permute-start.67
  1083.8 10.2 collective-permute-start.48
  1102.2 5.2 collective-permute-start.44
  1107.3 4.0 collective-permute-start.43
  1132.1 15.0 collective-permute-start.34
  1147.1 13.1 collective-permute-start.33
  1160.3 13.1 collective-permute-start.32
  1173.4 13.1 collective-permute-start.31
  1186.6 13.1 collective-permute-start.30
  1199.7 13.1 collective-permute-start.29
  1212.9 13.1 collective-permute-start.28
  1226.0 13.1 collective-permute-start.27
  1239.2 13.1 collective-permute-start.26
  1252.3 13.1 collective-permute-start.25
  1265.5 13.1 collective-permute-start.24
  1278.6 13.1 collective-permute-start.23
  1291.8 13.1 collective-permute-start.22
  1304.9 13.1 collective-permute-start.21
  1318.1 13.1 collective-permute-start.20
  1331.2 13.1 collective-permute-start.19
  1344.4 13.1 collective-permute-start.18
  1357.5 13.1 collective-permute-start.17
  1370.7 13.1 collective-permute-start.16
  1383.8 13.1 collective-permute-start.15
  1397.0 13.1 collective-permute-start.14
  1410.1 13.1 collective-permute-start.13
  1423.3 13.1 collective-permute-start.12
  1436.4 13.1 collective-permute-start.11
  1449.6 13.1 collective-permute-start.10
  1462.7 13.1 collective-permute-start.9
  1475.9 13.1 collective-permute-start.8
  1489.0 13.1 collective-permute-start.7
  1502.2 13.1 collective-permute-start.6
  1515.3 13.1 collective-permute-start.5
  1528.5 13.3 collective-permute-start.4
  1542.2 12.0 collective-permute-done.4
  1554.2 97.0 %concatenate.41 = f32[518,1536]{1,0:T(8,128)} concatenate(f32[6,1536]{1,0:T(8,128)S(1)} %collective-permute-done.67, f32[8,1536]{1,0:T(8,128)S(1)} %collective-permute-done.66, f32[8,1536]{1,0:T(8,128)S(1)} %collective-permute-done.65, f32[8,1536]{1,0:T(8,128)S(1)} %collective-permute-done.64, f32[8,1536]{1,0:T(8,128)S(1)} %collective-permute-done.63, ...), dimensions={0} | concatenate | bytes 6365184
  1652.9 8.4 reshape.28
  1661.3 4.1 fusion.99
  1665.4 72.6 %all-reduce.2 = (f32[1536]{0:T(1024)}, f32[1536]{0:T(1024)S(1)}) all-reduce(f32[1536]{0:T(1024)S(1)} %get-tuple-element.40, f32[1536]{0:T(1024)S(1)} %get-tuple-element.39), channel_id=1, replica_groups=mesh['dp'=4,'seq'=64] {'dp','seq'}, use_global_device_ids=true, to_apply=%region_8.9 | all-reduce | flops 3072 | bytes 24576 | tf_op jit(solution)/shard_map/psum | solution.py:69
  1751.2 4.4 fusion.94
  1755.6 244.2 %all-reduce.5.cloned.1.call-done = f32[31,1536]{1,0:T(8,128)} async-done(((f32[31,1536]{1,0:T(8,128)}), f32[31,1536]{1,0:T(8,128)}) %all-reduce.5.cloned.1.call-update) | async-done | bytes 190480 | tf_op jit(solution)/shard_map/psum | solution.py:86
  (282 shorter events, 91.4 us)
Async XLA Ops:
  7.2 1645.7 %all-gather.3.cloned.1.call-start = ((), (), s32[]{:S(2)}) async-start(), calls=%async_computation.1 | async-start | bytes 6316032 | tf_op jit(solution)/shard_map/all_gather | solution.py:58
  7.9 1991.8 %all-reduce.5.cloned.1.call-start = ((), (), s32[]{:S(2)}) async-start(), calls=%async_computation | async-start | bytes 393216 | tf_op jit(solution)/shard_map/psum | solution.py:86
  998.0 59.9 %collective-permute-start.66 = (f32[8,1536]{1,0:T(8,128)S(1)}, f32[8,1536]{1,0:T(8,128)S(1)}, u32[]{:S(2)}, u32[]{:S(2)}) collective-permute-start(f32[8,1536]{1,0:T(8,128)S(1)} %fusion), channel_id=1, source_target_pairs={{0,63},{1,64},{2,65},{3,66},{4,67},{5,68},{6,69},{7,70},{8,71},{9,... | collective-permute-start | bytes 147464
  1075.3 18.7 collective-permute-start.52
  1077.2 18.7 collective-permute-start.51
  1079.2 19.2 collective-permute-start.50
  1081.1 21.0 %collective-permute-start.49 = (f32[8,1536]{1,0:T(8,128)S(1)}, f32[8,1536]{1,0:T(8,128)S(1)}, u32[]{:S(2)}, u32[]{:S(2)}) collective-permute-start(f32[8,1536]{1,0:T(8,128)S(1)} %fusion), channel_id=1, source_target_pairs={{0,46},{1,47},{2,48},{3,49},{4,50},{5,51},{6,52},{7,53},{8,54},{9,... | collective-permute-start | bytes 147464
  1083.8 23.6 %collective-permute-start.48 = (f32[8,1536]{1,0:T(8,128)S(1)}, f32[8,1536]{1,0:T(8,128)S(1)}, u32[]{:S(2)}, u32[]{:S(2)}) collective-permute-start(f32[8,1536]{1,0:T(8,128)S(1)} %fusion), channel_id=1, source_target_pairs={{0,45},{1,46},{2,47},{3,48},{4,49},{5,50},{6,51},{7,52},{8,53},{9,... | collective-permute-start | bytes 147464
  1094.0 17.3 collective-permute-start.47
  1095.9 18.0 collective-permute-start.46
  1098.3 19.2 collective-permute-start.45
  1102.2 17.3 collective-permute-start.44
  1107.3 14.1 collective-permute-start.43
  1121.5 25.6 %collective-permute-start.38 = (f32[8,1536]{1,0:T(8,128)S(1)}, f32[8,1536]{1,0:T(8,128)S(1)}, u32[]{:S(2)}, u32[]{:S(2)}) collective-permute-start(f32[8,1536]{1,0:T(8,128)S(1)} %fusion), channel_id=1, source_target_pairs={{0,35},{1,36},{2,37},{3,38},{4,39},{5,40},{6,41},{7,42},{8,43},{9,... | collective-permute-start | bytes 147464
  1123.4 36.8 %collective-permute-start.37 = (f32[8,1536]{1,0:T(8,128)S(1)}, f32[8,1536]{1,0:T(8,128)S(1)}, u32[]{:S(2)}, u32[]{:S(2)}) collective-permute-start(f32[8,1536]{1,0:T(8,128)S(1)} %fusion), channel_id=1, source_target_pairs={{0,34},{1,35},{2,36},{3,37},{4,38},{5,39},{6,40},{7,41},{8,42},{9,... | collective-permute-start | bytes 147464
  1127.1 46.3 %collective-permute-start.36 = (f32[8,1536]{1,0:T(8,128)S(1)}, f32[8,1536]{1,0:T(8,128)S(1)}, u32[]{:S(2)}, u32[]{:S(2)}) collective-permute-start(f32[8,1536]{1,0:T(8,128)S(1)} %fusion), channel_id=1, source_target_pairs={{0,33},{1,34},{2,35},{3,36},{4,37},{5,38},{6,39},{7,40},{8,41},{9,... | collective-permute-start | bytes 147464
  1130.0 56.5 %collective-permute-start.35 = (f32[8,1536]{1,0:T(8,128)S(1)}, f32[8,1536]{1,0:T(8,128)S(1)}, u32[]{:S(2)}, u32[]{:S(2)}) collective-permute-start(f32[8,1536]{1,0:T(8,128)S(1)} %fusion), channel_id=1, source_target_pairs={{0,32},{1,33},{2,34},{3,35},{4,36},{5,37},{6,38},{7,39},{8,40},{9,... | collective-permute-start | bytes 147464
  1132.1 67.6 %collective-permute-start.34 = (f32[8,1536]{1,0:T(8,128)S(1)}, f32[8,1536]{1,0:T(8,128)S(1)}, u32[]{:S(2)}, u32[]{:S(2)}) collective-permute-start(f32[8,1536]{1,0:T(8,128)S(1)} %fusion), channel_id=1, source_target_pairs={{0,31},{1,32},{2,33},{3,34},{4,35},{5,36},{6,37},{7,38},{8,39},{9,... | collective-permute-start | bytes 147464
  1147.1 65.7 %collective-permute-start.33 = (f32[8,1536]{1,0:T(8,128)S(1)}, f32[8,1536]{1,0:T(8,128)S(1)}, u32[]{:S(2)}, u32[]{:S(2)}) collective-permute-start(f32[8,1536]{1,0:T(8,128)S(1)} %fusion), channel_id=1, source_target_pairs={{0,30},{1,31},{2,32},{3,33},{4,34},{5,35},{6,36},{7,37},{8,38},{9,... | collective-permute-start | bytes 147464
  1160.3 65.7 %collective-permute-start.32 = (f32[8,1536]{1,0:T(8,128)S(1)}, f32[8,1536]{1,0:T(8,128)S(1)}, u32[]{:S(2)}, u32[]{:S(2)}) collective-permute-start(f32[8,1536]{1,0:T(8,128)S(1)} %fusion), channel_id=1, source_target_pairs={{0,29},{1,30},{2,31},{3,32},{4,33},{5,34},{6,35},{7,36},{8,37},{9,... | collective-permute-start | bytes 147464
  1173.4 65.7 %collective-permute-start.31 = (f32[8,1536]{1,0:T(8,128)S(1)}, f32[8,1536]{1,0:T(8,128)S(1)}, u32[]{:S(2)}, u32[]{:S(2)}) collective-permute-start(f32[8,1536]{1,0:T(8,128)S(1)} %fusion), channel_id=1, source_target_pairs={{0,28},{1,29},{2,30},{3,31},{4,32},{5,33},{6,34},{7,35},{8,36},{9,... | collective-permute-start | bytes 147464
  1186.6 65.7 %collective-permute-start.30 = (f32[8,1536]{1,0:T(8,128)S(1)}, f32[8,1536]{1,0:T(8,128)S(1)}, u32[]{:S(2)}, u32[]{:S(2)}) collective-permute-start(f32[8,1536]{1,0:T(8,128)S(1)} %fusion), channel_id=1, source_target_pairs={{0,27},{1,28},{2,29},{3,30},{4,31},{5,32},{6,33},{7,34},{8,35},{9,... | collective-permute-start | bytes 147464
  1199.7 65.7 %collective-permute-start.29 = (f32[8,1536]{1,0:T(8,128)S(1)}, f32[8,1536]{1,0:T(8,128)S(1)}, u32[]{:S(2)}, u32[]{:S(2)}) collective-permute-start(f32[8,1536]{1,0:T(8,128)S(1)} %fusion), channel_id=1, source_target_pairs={{0,26},{1,27},{2,28},{3,29},{4,30},{5,31},{6,32},{7,33},{8,34},{9,... | collective-permute-start | bytes 147464
  1212.9 65.7 %collective-permute-start.28 = (f32[8,1536]{1,0:T(8,128)S(1)}, f32[8,1536]{1,0:T(8,128)S(1)}, u32[]{:S(2)}, u32[]{:S(2)}) collective-permute-start(f32[8,1536]{1,0:T(8,128)S(1)} %fusion), channel_id=1, source_target_pairs={{0,25},{1,26},{2,27},{3,28},{4,29},{5,30},{6,31},{7,32},{8,33},{9,... | collective-permute-start | bytes 147464
  1226.0 65.7 %collective-permute-start.27 = (f32[8,1536]{1,0:T(8,128)S(1)}, f32[8,1536]{1,0:T(8,128)S(1)}, u32[]{:S(2)}, u32[]{:S(2)}) collective-permute-start(f32[8,1536]{1,0:T(8,128)S(1)} %fusion), channel_id=1, source_target_pairs={{0,24},{1,25},{2,26},{3,27},{4,28},{5,29},{6,30},{7,31},{8,32},{9,... | collective-permute-start | bytes 147464
  1239.2 65.7 %collective-permute-start.26 = (f32[8,1536]{1,0:T(8,128)S(1)}, f32[8,1536]{1,0:T(8,128)S(1)}, u32[]{:S(2)}, u32[]{:S(2)}) collective-permute-start(f32[8,1536]{1,0:T(8,128)S(1)} %fusion), channel_id=1, source_target_pairs={{0,23},{1,24},{2,25},{3,26},{4,27},{5,28},{6,29},{7,30},{8,31},{9,... | collective-permute-start | bytes 147464
  1252.3 65.7 %collective-permute-start.25 = (f32[8,1536]{1,0:T(8,128)S(1)}, f32[8,1536]{1,0:T(8,128)S(1)}, u32[]{:S(2)}, u32[]{:S(2)}) collective-permute-start(f32[8,1536]{1,0:T(8,128)S(1)} %fusion), channel_id=1, source_target_pairs={{0,22},{1,23},{2,24},{3,25},{4,26},{5,27},{6,28},{7,29},{8,30},{9,... | collective-permute-start | bytes 147464
  1265.5 65.7 %collective-permute-start.24 = (f32[8,1536]{1,0:T(8,128)S(1)}, f32[8,1536]{1,0:T(8,128)S(1)}, u32[]{:S(2)}, u32[]{:S(2)}) collective-permute-start(f32[8,1536]{1,0:T(8,128)S(1)} %fusion), channel_id=1, source_target_pairs={{0,21},{1,22},{2,23},{3,24},{4,25},{5,26},{6,27},{7,28},{8,29},{9,... | collective-permute-start | bytes 147464
  1278.6 65.7 %collective-permute-start.23 = (f32[8,1536]{1,0:T(8,128)S(1)}, f32[8,1536]{1,0:T(8,128)S(1)}, u32[]{:S(2)}, u32[]{:S(2)}) collective-permute-start(f32[8,1536]{1,0:T(8,128)S(1)} %fusion), channel_id=1, source_target_pairs={{0,20},{1,21},{2,22},{3,23},{4,24},{5,25},{6,26},{7,27},{8,28},{9,... | collective-permute-start | bytes 147464
  1291.8 65.7 %collective-permute-start.22 = (f32[8,1536]{1,0:T(8,128)S(1)}, f32[8,1536]{1,0:T(8,128)S(1)}, u32[]{:S(2)}, u32[]{:S(2)}) collective-permute-start(f32[8,1536]{1,0:T(8,128)S(1)} %fusion), channel_id=1, source_target_pairs={{0,19},{1,20},{2,21},{3,22},{4,23},{5,24},{6,25},{7,26},{8,27},{9,... | collective-permute-start | bytes 147464
  1304.9 65.7 %collective-permute-start.21 = (f32[8,1536]{1,0:T(8,128)S(1)}, f32[8,1536]{1,0:T(8,128)S(1)}, u32[]{:S(2)}, u32[]{:S(2)}) collective-permute-start(f32[8,1536]{1,0:T(8,128)S(1)} %fusion), channel_id=1, source_target_pairs={{0,18},{1,19},{2,20},{3,21},{4,22},{5,23},{6,24},{7,25},{8,26},{9,... | collective-permute-start | bytes 147464
  1318.1 65.7 %collective-permute-start.20 = (f32[8,1536]{1,0:T(8,128)S(1)}, f32[8,1536]{1,0:T(8,128)S(1)}, u32[]{:S(2)}, u32[]{:S(2)}) collective-permute-start(f32[8,1536]{1,0:T(8,128)S(1)} %fusion), channel_id=1, source_target_pairs={{0,17},{1,18},{2,19},{3,20},{4,21},{5,22},{6,23},{7,24},{8,25},{9,... | collective-permute-start | bytes 147464
  1331.2 65.7 %collective-permute-start.19 = (f32[8,1536]{1,0:T(8,128)S(1)}, f32[8,1536]{1,0:T(8,128)S(1)}, u32[]{:S(2)}, u32[]{:S(2)}) collective-permute-start(f32[8,1536]{1,0:T(8,128)S(1)} %fusion), channel_id=1, source_target_pairs={{0,16},{1,17},{2,18},{3,19},{4,20},{5,21},{6,22},{7,23},{8,24},{9,... | collective-permute-start | bytes 147464
  1344.4 65.7 %collective-permute-start.18 = (f32[8,1536]{1,0:T(8,128)S(1)}, f32[8,1536]{1,0:T(8,128)S(1)}, u32[]{:S(2)}, u32[]{:S(2)}) collective-permute-start(f32[8,1536]{1,0:T(8,128)S(1)} %fusion), channel_id=1, source_target_pairs={{0,15},{1,16},{2,17},{3,18},{4,19},{5,20},{6,21},{7,22},{8,23},{9,... | collective-permute-start | bytes 147464
  1357.5 65.7 %collective-permute-start.17 = (f32[8,1536]{1,0:T(8,128)S(1)}, f32[8,1536]{1,0:T(8,128)S(1)}, u32[]{:S(2)}, u32[]{:S(2)}) collective-permute-start(f32[8,1536]{1,0:T(8,128)S(1)} %fusion), channel_id=1, source_target_pairs={{0,14},{1,15},{2,16},{3,17},{4,18},{5,19},{6,20},{7,21},{8,22},{9,... | collective-permute-start | bytes 147464
  1370.7 65.7 %collective-permute-start.16 = (f32[8,1536]{1,0:T(8,128)S(1)}, f32[8,1536]{1,0:T(8,128)S(1)}, u32[]{:S(2)}, u32[]{:S(2)}) collective-permute-start(f32[8,1536]{1,0:T(8,128)S(1)} %fusion), channel_id=1, source_target_pairs={{0,13},{1,14},{2,15},{3,16},{4,17},{5,18},{6,19},{7,20},{8,21},{9,... | collective-permute-start | bytes 147464
  1383.8 65.7 %collective-permute-start.15 = (f32[8,1536]{1,0:T(8,128)S(1)}, f32[8,1536]{1,0:T(8,128)S(1)}, u32[]{:S(2)}, u32[]{:S(2)}) collective-permute-start(f32[8,1536]{1,0:T(8,128)S(1)} %fusion), channel_id=1, source_target_pairs={{0,12},{1,13},{2,14},{3,15},{4,16},{5,17},{6,18},{7,19},{8,20},{9,... | collective-permute-start | bytes 147464
  1397.0 65.7 %collective-permute-start.14 = (f32[8,1536]{1,0:T(8,128)S(1)}, f32[8,1536]{1,0:T(8,128)S(1)}, u32[]{:S(2)}, u32[]{:S(2)}) collective-permute-start(f32[8,1536]{1,0:T(8,128)S(1)} %fusion), channel_id=1, source_target_pairs={{0,11},{1,12},{2,13},{3,14},{4,15},{5,16},{6,17},{7,18},{8,19},{9,... | collective-permute-start | bytes 147464
  1410.1 65.7 %collective-permute-start.13 = (f32[8,1536]{1,0:T(8,128)S(1)}, f32[8,1536]{1,0:T(8,128)S(1)}, u32[]{:S(2)}, u32[]{:S(2)}) collective-permute-start(f32[8,1536]{1,0:T(8,128)S(1)} %fusion), channel_id=1, source_target_pairs={{0,10},{1,11},{2,12},{3,13},{4,14},{5,15},{6,16},{7,17},{8,18},{9,... | collective-permute-start | bytes 147464
  1423.3 65.7 %collective-permute-start.12 = (f32[8,1536]{1,0:T(8,128)S(1)}, f32[8,1536]{1,0:T(8,128)S(1)}, u32[]{:S(2)}, u32[]{:S(2)}) collective-permute-start(f32[8,1536]{1,0:T(8,128)S(1)} %fusion), channel_id=1, source_target_pairs={{0,9},{1,10},{2,11},{3,12},{4,13},{5,14},{6,15},{7,16},{8,17},{9,1... | collective-permute-start | bytes 147464
  1436.4 65.7 %collective-permute-start.11 = (f32[8,1536]{1,0:T(8,128)S(1)}, f32[8,1536]{1,0:T(8,128)S(1)}, u32[]{:S(2)}, u32[]{:S(2)}) collective-permute-start(f32[8,1536]{1,0:T(8,128)S(1)} %fusion), channel_id=1, source_target_pairs={{0,8},{1,9},{2,10},{3,11},{4,12},{5,13},{6,14},{7,15},{8,16},{9,17... | collective-permute-start | bytes 147464
  1449.6 65.7 %collective-permute-start.10 = (f32[8,1536]{1,0:T(8,128)S(1)}, f32[8,1536]{1,0:T(8,128)S(1)}, u32[]{:S(2)}, u32[]{:S(2)}) collective-permute-start(f32[8,1536]{1,0:T(8,128)S(1)} %fusion), channel_id=1, source_target_pairs={{0,7},{1,8},{2,9},{3,10},{4,11},{5,12},{6,13},{7,14},{8,15},{9,16}... | collective-permute-start | bytes 147464
  1462.7 65.7 %collective-permute-start.9 = (f32[8,1536]{1,0:T(8,128)S(1)}, f32[8,1536]{1,0:T(8,128)S(1)}, u32[]{:S(2)}, u32[]{:S(2)}) collective-permute-start(f32[8,1536]{1,0:T(8,128)S(1)} %fusion), channel_id=1, source_target_pairs={{0,6},{1,7},{2,8},{3,9},{4,10},{5,11},{6,12},{7,13},{8,14},{9,15},... | collective-permute-start | bytes 147464
  1475.9 66.3 %collective-permute-start.8 = (f32[8,1536]{1,0:T(8,128)S(1)}, f32[8,1536]{1,0:T(8,128)}, u32[]{:S(2)}, u32[]{:S(2)}) collective-permute-start(f32[8,1536]{1,0:T(8,128)S(1)} %fusion), channel_id=1, source_target_pairs={{0,5},{1,6},{2,7},{3,8},{4,9},{5,10},{6,11},{7,12},{8,13},{9,14},{... | collective-permute-start | bytes 147464
  1489.0 53.1 %collective-permute-start.7 = (f32[8,1536]{1,0:T(8,128)S(1)}, f32[8,1536]{1,0:T(8,128)}, u32[]{:S(2)}, u32[]{:S(2)}) collective-permute-start(f32[8,1536]{1,0:T(8,128)S(1)} %fusion), channel_id=1, source_target_pairs={{0,4},{1,5},{2,6},{3,7},{4,8},{5,9},{6,10},{7,11},{8,12},{9,13},{1... | collective-permute-start | bytes 147464
  1502.2 40.0 %collective-permute-start.6 = (f32[8,1536]{1,0:T(8,128)S(1)}, f32[8,1536]{1,0:T(8,128)}, u32[]{:S(2)}, u32[]{:S(2)}) collective-permute-start(f32[8,1536]{1,0:T(8,128)S(1)} %fusion), channel_id=1, source_target_pairs={{0,3},{1,4},{2,5},{3,6},{4,7},{5,8},{6,9},{7,10},{8,11},{9,12},{10... | collective-permute-start | bytes 147464
  1515.3 26.9 %collective-permute-start.5 = (f32[8,1536]{1,0:T(8,128)S(1)}, f32[8,1536]{1,0:T(8,128)}, u32[]{:S(2)}, u32[]{:S(2)}) collective-permute-start(f32[8,1536]{1,0:T(8,128)S(1)} %fusion), channel_id=1, source_target_pairs={{0,2},{1,3},{2,4},{3,5},{4,6},{5,7},{6,8},{7,9},{8,10},{9,11},{10,... | collective-permute-start | bytes 147464
  1528.5 25.7 %collective-permute-start.4 = (f32[8,1536]{1,0:T(8,128)S(1)}, f32[8,1536]{1,0:T(8,128)}, u32[]{:S(2)}, u32[]{:S(2)}) collective-permute-start(f32[8,1536]{1,0:T(8,128)S(1)} %fusion), channel_id=1, source_target_pairs={{0,1},{1,2},{2,3},{3,4},{4,5},{5,6},{6,7},{7,8},{8,9},{9,10},{10,1... | collective-permute-start | bytes 147464
  (85 other events, 9629.2 us)
Sparse Core Ops, SparseCore 0:
  9.9 738.2 all-gather.2
  1751.2 248.4 all-reduce.4
where the time goes:
time: 2010 us
  blocking collectives  1040 us (52%)
  starting transfers between devices  550 us (27%)
  waiting for transfers between devices  259 us (13%)
  local copies, waits for them, and re-layouts  115 us (6%)
    unnamed x1, blocking collectives  808 us
    unnamed x64, starting transfers between devices  541 us
    psum x1, waiting for transfers between devices, on_device(): kernel_grad = lax.psum(jnp.stack(tap_rows), ('dp', 'seq'))  244 us
    unnamed x130, local copies, waits for them, and re-layouts  108 us
    psum x1, blocking collectives, on_device(): lax.psum(jnp.sum(jnp.where(valid, conv_out, 0.0), axis=0), ('dp', 'seq'))  85.3 us
    psum x1, blocking collectives, on_device(): spread = lax.psum(jnp.sum(deviation * deviation, axis=0), ('dp', 'seq'))  73.7 us
    psum x1, blocking collectives, on_device(): lax.psum((jnp.sum(scaled_grad * standard, axis=0), jnp.sum(scaled_grad, a...  72.6 us
  transfers between devices with their start and end apart: 70, of which 3 were waited for; matrix products, arithmetic and copies ran while one was open for 46% of the time, Pallas kernels for 0%

commit v1 on v0

--- a/solution.py
+++ b/solution.py
@@ -67,7 +67,8 @@
     module_out = jnp.where(valid, product, 0.0).astype(jnp.bfloat16)
     scaled_grad = hidden_grad * logistic * (1.0 + scaled * (1.0 - logistic))
     gain_grad, bias_grad = lax.psum(
-        (jnp.sum(scaled_grad * standard, axis=0), jnp.sum(scaled_grad, axis=0)), ("dp", "seq")
+        lax.psum((jnp.sum(scaled_grad * standard, axis=0), jnp.sum(scaled_grad, axis=0)), "dp"),
+        "seq",
     )
     conv_grad = jnp.where(
         valid,

time: 2010 us -> 2340 us (1.16)
  blocking collectives: 1040 us -> 1280 us
  waiting for transfers between devices: 259 us -> 314 us
  starting transfers between devices: 550 us -> 580 us
    psum x0 -> x1, blocking collectives: none -> 315 us  [on_device(): lax.psum(lax.psum((jnp.sum(scaled_grad * standard, axis=0), jnp.sum(scale...]
    psum x1, blocking collectives: 72.6 us -> 9.46 us  [on_device(): lax.psum((jnp.sum(scaled_grad * standard, axis=0), jnp.sum(scaled_grad, a...]
    psum x1, waiting for transfers between devices: 244 us -> 300 us  [on_device(): kernel_grad = lax.psum(jnp.stack(tap_rows), ('dp', 'seq'))]
    unnamed x64, starting transfers between devices: 541 us -> 571 us
  transfers between devices with their start and end apart: 70 -> 70, of which waited for: 3 -> 3; matrix products, arithmetic and copies ran while one was open for 46% -> 39% of each run, Pallas kernels for 0% -> 0%
where the time goes in v1:
time: 2340 us
  blocking collectives  1280 us (55%)
  starting transfers between devices  580 us (25%)
  waiting for transfers between devices  314 us (13%)
  local copies, waits for them, and re-layouts  115 us (5%)
    unnamed x1, blocking collectives  799 us
    unnamed x64, starting transfers between devices  571 us
    psum x1, blocking collectives, on_device(): lax.psum(lax.psum((jnp.sum(scaled_grad * standard, axis=0), jnp.sum(scale...  315 us
    psum x1, waiting for transfers between devices, on_device(): kernel_grad = lax.psum(jnp.stack(tap_rows), ('dp', 'seq'))  300 us
    unnamed x130, local copies, waits for them, and re-layouts  108 us
    psum x1, blocking collectives, on_device(): lax.psum(jnp.sum(jnp.where(valid, conv_out, 0.0), axis=0), ('dp', 'seq'))  85.3 us
    psum x1, blocking collectives, on_device(): spread = lax.psum(jnp.sum(deviation * deviation, axis=0), ('dp', 'seq'))  73.7 us
  transfers between devices with their start and end apart: 70, of which 3 were waited for; matrix products, arithmetic and copies ran while one was open for 39% of the time, Pallas kernels for 0%

profile of v1, /device:TPU:1, one launch (start us, length us, event | category | flops | bytes accessed | tf_op | source)
XLA Modules:
  0.0 2336.2 jit_solution(9792577715766506649)
XLA Ops:
  12.3 4.6 collective-permute-start
  25.6 85.3 %psum.49 = f32[1536]{0:T(1024)S(1)} all-reduce(f32[1536]{0:T(1024)S(1)} %get-tuple-element.80), channel_id=1, replica_groups=mesh['dp'=4,'seq'=64] {'dp','seq'}, use_global_device_ids=true, to_apply=%region_1.2 | all-reduce | flops 1536 | bytes 12288 | tf_op jit(solution)/shard_map/psum | solution.py:44
  111.1 73.7 %psum.50 = f32[1536]{0:T(1024)S(1)} all-reduce(f32[1536]{0:T(1024)S(1)} %multiply_reduce_fusion.32), channel_id=1, replica_groups=mesh['dp'=4,'seq'=64] {'dp','seq'}, use_global_device_ids=true, to_apply=%region_4.5 | all-reduce | flops 1536 | bytes 12288 | tf_op jit(solution)/shard_map/psum | solution.py:47
  184.9 5.1 fusion.95
  190.0 798.7 %fusion = f32[8,1536]{1,0:T(8,128)S(1)} fusion(f32[1536,1536]{1,0:T(8,128)} %fusion.95), kind=kCustom, calls=%all-reduce-scatter | all-reduce-scatter fusion | flops 3145729 | bytes 9486336
  988.7 57.5 %collective-permute-start.66 = (f32[8,1536]{1,0:T(8,128)S(1)}, f32[8,1536]{1,0:T(8,128)S(1)}, u32[]{:S(2)}, u32[]{:S(2)}) collective-permute-start(f32[8,1536]{1,0:T(8,128)S(1)} %fusion), channel_id=1, source_target_pairs={{0,63},{1,64},{2,65},{3,66},{4,67},{5,68},{6,69},{7,70},{8,71},{9,... | collective-permute-start | bytes 147464
  1084.0 9.1 collective-permute-start.48
  1097.7 4.9 collective-permute-start.45
  1102.6 5.9 collective-permute-start.44
  1126.5 14.6 collective-permute-start.36
  1141.1 13.1 collective-permute-start.35
  1154.2 13.1 collective-permute-start.34
  1167.4 13.1 collective-permute-start.33
  1180.5 13.1 collective-permute-start.32
  1193.7 13.1 collective-permute-start.31
  1206.8 13.1 collective-permute-start.30
  1220.0 13.1 collective-permute-start.29
  1233.1 13.1 collective-permute-start.28
  1246.3 13.1 collective-permute-start.27
  1259.4 13.1 collective-permute-start.26
  1272.6 13.1 collective-permute-start.25
  1285.7 13.1 collective-permute-start.24
  1298.9 13.1 collective-permute-start.23
  1312.0 13.1 collective-permute-start.22
  1325.2 13.1 collective-permute-start.21
  1338.3 13.1 collective-permute-start.20
  1351.5 13.1 collective-permute-start.19
  1364.6 13.1 collective-permute-start.18
  1377.8 13.1 collective-permute-start.17
  1390.9 13.1 collective-permute-start.16
  1404.1 13.1 collective-permute-start.15
  1417.2 13.1 collective-permute-start.14
  1430.4 13.1 collective-permute-start.13
  1443.5 13.1 collective-permute-start.12
  1456.7 13.1 collective-permute-start.11
  1469.8 13.1 collective-permute-start.10
  1483.0 13.1 collective-permute-start.9
  1496.1 13.1 collective-permute-start.8
  1509.3 13.1 collective-permute-start.7
  1522.4 13.1 collective-permute-start.6
  1535.6 13.1 collective-permute-start.5
  1548.7 13.3 collective-permute-start.4
  1562.4 12.0 collective-permute-done.4
  1574.5 97.0 %concatenate.41 = f32[518,1536]{1,0:T(8,128)} concatenate(f32[6,1536]{1,0:T(8,128)S(1)} %collective-permute-done.67, f32[8,1536]{1,0:T(8,128)S(1)} %collective-permute-done.66, f32[8,1536]{1,0:T(8,128)S(1)} %collective-permute-done.65, f32[8,1536]{1,0:T(8,128)S(1)} %collective-permute-done.64, f32[8,1536]{1,0:T(8,128)S(1)} %collective-permute-done.63, ...), dimensions={0} | concatenate | bytes 6365184
  1673.1 8.4 reshape.28
  1685.6 9.5 all-reduce.3
  1695.1 315.0 %all-reduce.2 = (f32[1536]{0:T(1024)}, f32[1536]{0:T(1024)S(1)}) all-reduce(f32[1536]{0:T(1024)S(1)} %get-tuple-element.74, f32[1536]{0:T(1024)S(1)} %get-tuple-element.75), channel_id=1, replica_groups=mesh['dp'=4,'seq'=64] {'seq'}, use_global_device_ids=true, to_apply=%region_10.11 | all-reduce | flops 3072 | bytes 24576 | tf_op jit(solution)/shard_map/psum | solution.py:69
  2027.3 300.4 %all-reduce.6.cloned.1.call-done = f32[31,1536]{1,0:T(8,128)} async-done(((f32[31,1536]{1,0:T(8,128)}), f32[31,1536]{1,0:T(8,128)}) %all-reduce.6.cloned.1.call-update) | async-done | bytes 190480 | tf_op jit(solution)/shard_map/psum | solution.py:87
  (283 shorter events, 97.3 us)
Async XLA Ops:
  7.2 1665.9 %all-gather.3.cloned.1.call-start = ((), (), s32[]{:S(2)}) async-start(), calls=%async_computation.1 | async-start | bytes 6316032 | tf_op jit(solution)/shard_map/all_gather | solution.py:58
  7.9 2319.8 %all-reduce.6.cloned.1.call-start = ((), (), s32[]{:S(2)}) async-start(), calls=%async_computation | async-start | bytes 393216 | tf_op jit(solution)/shard_map/psum | solution.py:87
  988.7 69.2 %collective-permute-start.66 = (f32[8,1536]{1,0:T(8,128)S(1)}, f32[8,1536]{1,0:T(8,128)S(1)}, u32[]{:S(2)}, u32[]{:S(2)}) collective-permute-start(f32[8,1536]{1,0:T(8,128)S(1)} %fusion), channel_id=1, source_target_pairs={{0,63},{1,64},{2,65},{3,66},{4,67},{5,68},{6,69},{7,70},{8,71},{9,... | collective-permute-start | bytes 147464
  1075.3 17.7 collective-permute-start.52
  1077.3 17.7 collective-permute-start.51
  1079.2 18.5 collective-permute-start.50
  1081.2 21.5 collective-permute-start.49
  1084.0 24.6 %collective-permute-start.48 = (f32[8,1536]{1,0:T(8,128)S(1)}, f32[8,1536]{1,0:T(8,128)S(1)}, u32[]{:S(2)}, u32[]{:S(2)}) collective-permute-start(f32[8,1536]{1,0:T(8,128)S(1)} %fusion), channel_id=1, source_target_pairs={{0,45},{1,46},{2,47},{3,48},{4,49},{5,50},{6,51},{7,52},{8,53},{9,... | collective-permute-start | bytes 147464
  1093.1 19.4 collective-permute-start.47
  1095.0 20.0 collective-permute-start.46
  1097.7 20.5 collective-permute-start.45
  1118.2 22.8 collective-permute-start.40
  1120.2 34.0 %collective-permute-start.39 = (f32[8,1536]{1,0:T(8,128)S(1)}, f32[8,1536]{1,0:T(8,128)S(1)}, u32[]{:S(2)}, u32[]{:S(2)}) collective-permute-start(f32[8,1536]{1,0:T(8,128)S(1)} %fusion), channel_id=1, source_target_pairs={{0,36},{1,37},{2,38},{3,39},{4,40},{5,41},{6,42},{7,43},{8,44},{9,... | collective-permute-start | bytes 147464
  1122.1 45.2 %collective-permute-start.38 = (f32[8,1536]{1,0:T(8,128)S(1)}, f32[8,1536]{1,0:T(8,128)S(1)}, u32[]{:S(2)}, u32[]{:S(2)}) collective-permute-start(f32[8,1536]{1,0:T(8,128)S(1)} %fusion), channel_id=1, source_target_pairs={{0,35},{1,36},{2,37},{3,38},{4,39},{5,40},{6,41},{7,42},{8,43},{9,... | collective-permute-start | bytes 147464
  1124.1 56.4 %collective-permute-start.37 = (f32[8,1536]{1,0:T(8,128)S(1)}, f32[8,1536]{1,0:T(8,128)S(1)}, u32[]{:S(2)}, u32[]{:S(2)}) collective-permute-start(f32[8,1536]{1,0:T(8,128)S(1)} %fusion), channel_id=1, source_target_pairs={{0,34},{1,35},{2,36},{3,37},{4,38},{5,39},{6,40},{7,41},{8,42},{9,... | collective-permute-start | bytes 147464
  1126.5 67.2 %collective-permute-start.36 = (f32[8,1536]{1,0:T(8,128)S(1)}, f32[8,1536]{1,0:T(8,128)S(1)}, u32[]{:S(2)}, u32[]{:S(2)}) collective-permute-start(f32[8,1536]{1,0:T(8,128)S(1)} %fusion), channel_id=1, source_target_pairs={{0,33},{1,34},{2,35},{3,36},{4,37},{5,38},{6,39},{7,40},{8,41},{9,... | collective-permute-start | bytes 147464
  1141.1 65.7 %collective-permute-start.35 = (f32[8,1536]{1,0:T(8,128)S(1)}, f32[8,1536]{1,0:T(8,128)S(1)}, u32[]{:S(2)}, u32[]{:S(2)}) collective-permute-start(f32[8,1536]{1,0:T(8,128)S(1)} %fusion), channel_id=1, source_target_pairs={{0,32},{1,33},{2,34},{3,35},{4,36},{5,37},{6,38},{7,39},{8,40},{9,... | collective-permute-start | bytes 147464
  1154.2 65.7 %collective-permute-start.34 = (f32[8,1536]{1,0:T(8,128)S(1)}, f32[8,1536]{1,0:T(8,128)S(1)}, u32[]{:S(2)}, u32[]{:S(2)}) collective-permute-start(f32[8,1536]{1,0:T(8,128)S(1)} %fusion), channel_id=1, source_target_pairs={{0,31},{1,32},{2,33},{3,34},{4,35},{5,36},{6,37},{7,38},{8,39},{9,... | collective-permute-start | bytes 147464
  1167.4 65.7 %collective-permute-start.33 = (f32[8,1536]{1,0:T(8,128)S(1)}, f32[8,1536]{1,0:T(8,128)S(1)}, u32[]{:S(2)}, u32[]{:S(2)}) collective-permute-start(f32[8,1536]{1,0:T(8,128)S(1)} %fusion), channel_id=1, source_target_pairs={{0,30},{1,31},{2,32},{3,33},{4,34},{5,35},{6,36},{7,37},{8,38},{9,... | collective-permute-start | bytes 147464
  1180.5 65.7 %collective-permute-start.32 = (f32[8,1536]{1,0:T(8,128)S(1)}, f32[8,1536]{1,0:T(8,128)S(1)}, u32[]{:S(2)}, u32[]{:S(2)}) collective-permute-start(f32[8,1536]{1,0:T(8,128)S(1)} %fusion), channel_id=1, source_target_pairs={{0,29},{1,30},{2,31},{3,32},{4,33},{5,34},{6,35},{7,36},{8,37},{9,... | collective-permute-start | bytes 147464
  1193.7 65.7 %collective-permute-start.31 = (f32[8,1536]{1,0:T(8,128)S(1)}, f32[8,1536]{1,0:T(8,128)S(1)}, u32[]{:S(2)}, u32[]{:S(2)}) collective-permute-start(f32[8,1536]{1,0:T(8,128)S(1)} %fusion), channel_id=1, source_target_pairs={{0,28},{1,29},{2,30},{3,31},{4,32},{5,33},{6,34},{7,35},{8,36},{9,... | collective-permute-start | bytes 147464
  1206.8 65.7 %collective-permute-start.30 = (f32[8,1536]{1,0:T(8,128)S(1)}, f32[8,1536]{1,0:T(8,128)S(1)}, u32[]{:S(2)}, u32[]{:S(2)}) collective-permute-start(f32[8,1536]{1,0:T(8,128)S(1)} %fusion), channel_id=1, source_target_pairs={{0,27},{1,28},{2,29},{3,30},{4,31},{5,32},{6,33},{7,34},{8,35},{9,... | collective-permute-start | bytes 147464
  1220.0 65.7 %collective-permute-start.29 = (f32[8,1536]{1,0:T(8,128)S(1)}, f32[8,1536]{1,0:T(8,128)S(1)}, u32[]{:S(2)}, u32[]{:S(2)}) collective-permute-start(f32[8,1536]{1,0:T(8,128)S(1)} %fusion), channel_id=1, source_target_pairs={{0,26},{1,27},{2,28},{3,29},{4,30},{5,31},{6,32},{7,33},{8,34},{9,... | collective-permute-start | bytes 147464
  1233.1 65.7 %collective-permute-start.28 = (f32[8,1536]{1,0:T(8,128)S(1)}, f32[8,1536]{1,0:T(8,128)S(1)}, u32[]{:S(2)}, u32[]{:S(2)}) collective-permute-start(f32[8,1536]{1,0:T(8,128)S(1)} %fusion), channel_id=1, source_target_pairs={{0,25},{1,26},{2,27},{3,28},{4,29},{5,30},{6,31},{7,32},{8,33},{9,... | collective-permute-start | bytes 147464
  1246.3 65.7 %collective-permute-start.27 = (f32[8,1536]{1,0:T(8,128)S(1)}, f32[8,1536]{1,0:T(8,128)S(1)}, u32[]{:S(2)}, u32[]{:S(2)}) collective-permute-start(f32[8,1536]{1,0:T(8,128)S(1)} %fusion), channel_id=1, source_target_pairs={{0,24},{1,25},{2,26},{3,27},{4,28},{5,29},{6,30},{7,31},{8,32},{9,... | collective-permute-start | bytes 147464
  1259.4 65.7 %collective-permute-start.26 = (f32[8,1536]{1,0:T(8,128)S(1)}, f32[8,1536]{1,0:T(8,128)S(1)}, u32[]{:S(2)}, u32[]{:S(2)}) collective-permute-start(f32[8,1536]{1,0:T(8,128)S(1)} %fusion), channel_id=1, source_target_pairs={{0,23},{1,24},{2,25},{3,26},{4,27},{5,28},{6,29},{7,30},{8,31},{9,... | collective-permute-start | bytes 147464
  1272.6 65.7 %collective-permute-start.25 = (f32[8,1536]{1,0:T(8,128)S(1)}, f32[8,1536]{1,0:T(8,128)S(1)}, u32[]{:S(2)}, u32[]{:S(2)}) collective-permute-start(f32[8,1536]{1,0:T(8,128)S(1)} %fusion), channel_id=1, source_target_pairs={{0,22},{1,23},{2,24},{3,25},{4,26},{5,27},{6,28},{7,29},{8,30},{9,... | collective-permute-start | bytes 147464
  1285.7 65.7 %collective-permute-start.24 = (f32[8,1536]{1,0:T(8,128)S(1)}, f32[8,1536]{1,0:T(8,128)S(1)}, u32[]{:S(2)}, u32[]{:S(2)}) collective-permute-start(f32[8,1536]{1,0:T(8,128)S(1)} %fusion), channel_id=1, source_target_pairs={{0,21},{1,22},{2,23},{3,24},{4,25},{5,26},{6,27},{7,28},{8,29},{9,... | collective-permute-start | bytes 147464
  1298.9 65.7 %collective-permute-start.23 = (f32[8,1536]{1,0:T(8,128)S(1)}, f32[8,1536]{1,0:T(8,128)S(1)}, u32[]{:S(2)}, u32[]{:S(2)}) collective-permute-start(f32[8,1536]{1,0:T(8,128)S(1)} %fusion), channel_id=1, source_target_pairs={{0,20},{1,21},{2,22},{3,23},{4,24},{5,25},{6,26},{7,27},{8,28},{9,... | collective-permute-start | bytes 147464
  1312.0 65.7 %collective-permute-start.22 = (f32[8,1536]{1,0:T(8,128)S(1)}, f32[8,1536]{1,0:T(8,128)S(1)}, u32[]{:S(2)}, u32[]{:S(2)}) collective-permute-start(f32[8,1536]{1,0:T(8,128)S(1)} %fusion), channel_id=1, source_target_pairs={{0,19},{1,20},{2,21},{3,22},{4,23},{5,24},{6,25},{7,26},{8,27},{9,... | collective-permute-start | bytes 147464
  1325.2 65.7 %collective-permute-start.21 = (f32[8,1536]{1,0:T(8,128)S(1)}, f32[8,1536]{1,0:T(8,128)S(1)}, u32[]{:S(2)}, u32[]{:S(2)}) collective-permute-start(f32[8,1536]{1,0:T(8,128)S(1)} %fusion), channel_id=1, source_target_pairs={{0,18},{1,19},{2,20},{3,21},{4,22},{5,23},{6,24},{7,25},{8,26},{9,... | collective-permute-start | bytes 147464
  1338.3 65.7 %collective-permute-start.20 = (f32[8,1536]{1,0:T(8,128)S(1)}, f32[8,1536]{1,0:T(8,128)S(1)}, u32[]{:S(2)}, u32[]{:S(2)}) collective-permute-start(f32[8,1536]{1,0:T(8,128)S(1)} %fusion), channel_id=1, source_target_pairs={{0,17},{1,18},{2,19},{3,20},{4,21},{5,22},{6,23},{7,24},{8,25},{9,... | collective-permute-start | bytes 147464
  1351.5 65.7 %collective-permute-start.19 = (f32[8,1536]{1,0:T(8,128)S(1)}, f32[8,1536]{1,0:T(8,128)S(1)}, u32[]{:S(2)}, u32[]{:S(2)}) collective-permute-start(f32[8,1536]{1,0:T(8,128)S(1)} %fusion), channel_id=1, source_target_pairs={{0,16},{1,17},{2,18},{3,19},{4,20},{5,21},{6,22},{7,23},{8,24},{9,... | collective-permute-start | bytes 147464
  1364.6 65.7 %collective-permute-start.18 = (f32[8,1536]{1,0:T(8,128)S(1)}, f32[8,1536]{1,0:T(8,128)S(1)}, u32[]{:S(2)}, u32[]{:S(2)}) collective-permute-start(f32[8,1536]{1,0:T(8,128)S(1)} %fusion), channel_id=1, source_target_pairs={{0,15},{1,16},{2,17},{3,18},{4,19},{5,20},{6,21},{7,22},{8,23},{9,... | collective-permute-start | bytes 147464
  1377.8 65.7 %collective-permute-start.17 = (f32[8,1536]{1,0:T(8,128)S(1)}, f32[8,1536]{1,0:T(8,128)S(1)}, u32[]{:S(2)}, u32[]{:S(2)}) collective-permute-start(f32[8,1536]{1,0:T(8,128)S(1)} %fusion), channel_id=1, source_target_pairs={{0,14},{1,15},{2,16},{3,17},{4,18},{5,19},{6,20},{7,21},{8,22},{9,... | collective-permute-start | bytes 147464
  1390.9 65.7 %collective-permute-start.16 = (f32[8,1536]{1,0:T(8,128)S(1)}, f32[8,1536]{1,0:T(8,128)S(1)}, u32[]{:S(2)}, u32[]{:S(2)}) collective-permute-start(f32[8,1536]{1,0:T(8,128)S(1)} %fusion), channel_id=1, source_target_pairs={{0,13},{1,14},{2,15},{3,16},{4,17},{5,18},{6,19},{7,20},{8,21},{9,... | collective-permute-start | bytes 147464
  1404.1 65.7 %collective-permute-start.15 = (f32[8,1536]{1,0:T(8,128)S(1)}, f32[8,1536]{1,0:T(8,128)S(1)}, u32[]{:S(2)}, u32[]{:S(2)}) collective-permute-start(f32[8,1536]{1,0:T(8,128)S(1)} %fusion), channel_id=1, source_target_pairs={{0,12},{1,13},{2,14},{3,15},{4,16},{5,17},{6,18},{7,19},{8,20},{9,... | collective-permute-start | bytes 147464
  1417.2 65.7 %collective-permute-start.14 = (f32[8,1536]{1,0:T(8,128)S(1)}, f32[8,1536]{1,0:T(8,128)S(1)}, u32[]{:S(2)}, u32[]{:S(2)}) collective-permute-start(f32[8,1536]{1,0:T(8,128)S(1)} %fusion), channel_id=1, source_target_pairs={{0,11},{1,12},{2,13},{3,14},{4,15},{5,16},{6,17},{7,18},{8,19},{9,... | collective-permute-start | bytes 147464
  1430.4 65.7 %collective-permute-start.13 = (f32[8,1536]{1,0:T(8,128)S(1)}, f32[8,1536]{1,0:T(8,128)S(1)}, u32[]{:S(2)}, u32[]{:S(2)}) collective-permute-start(f32[8,1536]{1,0:T(8,128)S(1)} %fusion), channel_id=1, source_target_pairs={{0,10},{1,11},{2,12},{3,13},{4,14},{5,15},{6,16},{7,17},{8,18},{9,... | collective-permute-start | bytes 147464
  1443.5 65.7 %collective-permute-start.12 = (f32[8,1536]{1,0:T(8,128)S(1)}, f32[8,1536]{1,0:T(8,128)S(1)}, u32[]{:S(2)}, u32[]{:S(2)}) collective-permute-start(f32[8,1536]{1,0:T(8,128)S(1)} %fusion), channel_id=1, source_target_pairs={{0,9},{1,10},{2,11},{3,12},{4,13},{5,14},{6,15},{7,16},{8,17},{9,1... | collective-permute-start | bytes 147464
  1456.7 65.7 %collective-permute-start.11 = (f32[8,1536]{1,0:T(8,128)S(1)}, f32[8,1536]{1,0:T(8,128)S(1)}, u32[]{:S(2)}, u32[]{:S(2)}) collective-permute-start(f32[8,1536]{1,0:T(8,128)S(1)} %fusion), channel_id=1, source_target_pairs={{0,8},{1,9},{2,10},{3,11},{4,12},{5,13},{6,14},{7,15},{8,16},{9,17... | collective-permute-start | bytes 147464
  1469.8 65.7 %collective-permute-start.10 = (f32[8,1536]{1,0:T(8,128)S(1)}, f32[8,1536]{1,0:T(8,128)S(1)}, u32[]{:S(2)}, u32[]{:S(2)}) collective-permute-start(f32[8,1536]{1,0:T(8,128)S(1)} %fusion), channel_id=1, source_target_pairs={{0,7},{1,8},{2,9},{3,10},{4,11},{5,12},{6,13},{7,14},{8,15},{9,16}... | collective-permute-start | bytes 147464
  1483.0 65.7 %collective-permute-start.9 = (f32[8,1536]{1,0:T(8,128)S(1)}, f32[8,1536]{1,0:T(8,128)S(1)}, u32[]{:S(2)}, u32[]{:S(2)}) collective-permute-start(f32[8,1536]{1,0:T(8,128)S(1)} %fusion), channel_id=1, source_target_pairs={{0,6},{1,7},{2,8},{3,9},{4,10},{5,11},{6,12},{7,13},{8,14},{9,15},... | collective-permute-start | bytes 147464
  1496.1 66.3 %collective-permute-start.8 = (f32[8,1536]{1,0:T(8,128)S(1)}, f32[8,1536]{1,0:T(8,128)}, u32[]{:S(2)}, u32[]{:S(2)}) collective-permute-start(f32[8,1536]{1,0:T(8,128)S(1)} %fusion), channel_id=1, source_target_pairs={{0,5},{1,6},{2,7},{3,8},{4,9},{5,10},{6,11},{7,12},{8,13},{9,14},{... | collective-permute-start | bytes 147464
  1509.3 53.1 %collective-permute-start.7 = (f32[8,1536]{1,0:T(8,128)S(1)}, f32[8,1536]{1,0:T(8,128)}, u32[]{:S(2)}, u32[]{:S(2)}) collective-permute-start(f32[8,1536]{1,0:T(8,128)S(1)} %fusion), channel_id=1, source_target_pairs={{0,4},{1,5},{2,6},{3,7},{4,8},{5,9},{6,10},{7,11},{8,12},{9,13},{1... | collective-permute-start | bytes 147464
  1522.4 40.0 %collective-permute-start.6 = (f32[8,1536]{1,0:T(8,128)S(1)}, f32[8,1536]{1,0:T(8,128)}, u32[]{:S(2)}, u32[]{:S(2)}) collective-permute-start(f32[8,1536]{1,0:T(8,128)S(1)} %fusion), channel_id=1, source_target_pairs={{0,3},{1,4},{2,5},{3,6},{4,7},{5,8},{6,9},{7,10},{8,11},{9,12},{10... | collective-permute-start | bytes 147464
  1535.6 26.9 %collective-permute-start.5 = (f32[8,1536]{1,0:T(8,128)S(1)}, f32[8,1536]{1,0:T(8,128)}, u32[]{:S(2)}, u32[]{:S(2)}) collective-permute-start(f32[8,1536]{1,0:T(8,128)S(1)} %fusion), channel_id=1, source_target_pairs={{0,2},{1,3},{2,4},{3,5},{4,6},{5,7},{6,8},{7,9},{8,10},{9,11},{10,... | collective-permute-start | bytes 147464
  1548.7 25.7 %collective-permute-start.4 = (f32[8,1536]{1,0:T(8,128)S(1)}, f32[8,1536]{1,0:T(8,128)}, u32[]{:S(2)}, u32[]{:S(2)}) collective-permute-start(f32[8,1536]{1,0:T(8,128)S(1)} %fusion), channel_id=1, source_target_pairs={{0,1},{1,2},{2,3},{3,4},{4,5},{5,6},{6,7},{7,8},{8,9},{9,10},{10,1... | collective-permute-start | bytes 147464
  (85 other events, 9718.4 us)
Sparse Core Ops, SparseCore 0:
  9.9 732.2 all-gather.2
  2022.9 304.7 all-reduce.5
